TPU v7x, 256 devices: a whole 4x4x8 slice. The times are simulated.
256 devices in a mesh: tup: 32 (over z, y), lang: 8 (over x, core).
Axes of the slice: x: 4, y: 4, z: 8, core: 2. Of those that a mesh axis runs over, the one named last changes fastest.
Arguments:
- counts: bfloat16 [8, 4096, 16384], P('lang', 'tup'), may hold values from 0 to 80
- lengths: int32 [8, 4096], P('lang', 'tup'), may hold values from 96 to 128, as said below
- tuple_map: int32 [8, 4096], P('lang', 'tup'), may hold values from 0 to 4095, as said below
- topic_mix: bfloat16 [4096, 256], P('tup'), may hold values from 0.049804688 to 5
- word_probs: bfloat16 [8, 16384, 256], P('lang', 'tup'), may hold values from 0.099609375 to 10
Outputs:
- mix_update: float32 [4096, 256], P('tup')
- word_update: float32 [8, 16384, 256], P('lang', 'tup')
Inputs may be any that keep to these rules, and one draw needn't show every extreme that they name: `lengths`: the first row of every language spans all 128 tiles. `tuple_map`: each language names every tuple once; the 128 rows of one index of tup hold exactly 4 tuples t of each value of t // 128.
All inputs are finite; a program needn't handle non-finite values.
Results may differ from a plain program's by a relative error of at most 0.0003.
Values may be sent and summed in bfloat16 or wider, within the bound.
No kernel may reach another device: no remote copies, remote signals or barrier semaphores. Data moves between devices by JAX's collectives and lax.ppermute only.
A program may use at most 128 MiB of HBM per device.

v0:
```python
import math
import jax
import jax.numpy as jnp
from jax import lax
from jax.sharding import PartitionSpec as P


def ratio_block(count_block, mix_block, word_block):
    expected = lax.dot_general(
        mix_block, word_block, (((1,), (1,)), ((), ())), preferred_element_type=jnp.float32
    )
    return count_block.astype(jnp.float32) / expected


def topic_term(ratios, word_block):
    return jnp.dot(ratios, word_block.astype(jnp.float32), precision=lax.Precision.HIGHEST)


def word_term(ratios, mix_rows):
    return lax.dot_general(
        ratios,
        mix_rows.astype(jnp.float32),
        (((0,), (0,)), ((), ())),
        precision=lax.Precision.HIGHEST,
    )


def ratio_pass(row_counts, mix_rows, word_local):
    shard_len = word_local.shape[0]
    topics = word_local.shape[1]
    vocab_size = shard_len * lax.axis_size("tup")
    topic_zero = jnp.zeros((row_counts.shape[0], topics), jnp.float32)
    shard_rows = lax.all_gather(word_local, "tup", axis=0, tiled=True)
    row_span = shard_rows.shape[0]
    block_len = math.gcd(row_span, 2048)

    def block_step(block_index, inner_pair):
        topic_sum, word_sum = inner_pair
        begin_row = block_index * block_len
        word_block = lax.dynamic_slice_in_dim(shard_rows, begin_row, block_len, 0)
        count_block = lax.dynamic_slice_in_dim(row_counts, begin_row, block_len, 1)
        ratios = ratio_block(count_block, mix_rows, word_block)
        topic_sum = topic_sum + topic_term(ratios, word_block)
        word_sum = lax.dynamic_update_slice_in_dim(
            word_sum, word_term(ratios, mix_rows), begin_row, 0
        )
        return (topic_sum, word_sum)

    topic_sum, word_sum = lax.fori_loop(
        0,
        row_span // block_len,
        block_step,
        (topic_zero, jnp.zeros((vocab_size, topics), jnp.float32)),
    )
    return (topic_sum, lax.psum_scatter(word_sum, "tup", scatter_dimension=0, tiled=True))


def on_device(counts, lengths, tuple_map, topic_mix, word_probs):
    count_rows = counts[0]
    tup_rows, vocab_size = count_rows.shape
    topics = topic_mix.shape[1]
    groups = lax.axis_size("tup")
    per_owner = tup_rows // groups
    tile_of = jnp.arange(vocab_size, dtype=jnp.int32) // 128
    live_counts = count_rows * (tile_of[None, :] < lengths[0][:, None]).astype(jnp.bfloat16)
    tuple_ids = tuple_map[0]
    word_local = word_probs[0]
    bucket_order = jnp.argsort(tuple_ids // tup_rows, stable=True)
    bucket_ids = tuple_ids[bucket_order].reshape(groups, per_owner)
    arrived = lax.all_to_all(
        live_counts[bucket_order].reshape(groups, per_owner, vocab_size),
        "tup",
        split_axis=0,
        concat_axis=0,
        tiled=True,
    ).reshape(tup_rows, vocab_size)
    arrived_ids = lax.all_to_all(
        bucket_ids, "tup", split_axis=0, concat_axis=0, tiled=True
    ).reshape(tup_rows)
    local_ids = arrived_ids % tup_rows
    mix_rows = topic_mix[local_ids]
    topic_sum, word_sum = ratio_pass(arrived, mix_rows, word_local)
    placed = jnp.zeros_like(topic_sum).at[local_ids].set(topic_sum)
    totals = lax.psum(placed, "lang")
    mixed = topic_mix.astype(jnp.float32) * totals
    mix_update = topics * mixed / jnp.sum(mixed, 1, keepdims=True)
    scaled = word_local.astype(jnp.float32) * word_sum
    column = lax.psum(jnp.sum(scaled, 0), "tup")
    word_update = (vocab_size * scaled / column[None, :])[None]
    return (mix_update, word_update)


def solution(mesh):
    return jax.shard_map(
        on_device,
        mesh=mesh,
        in_specs=(
            P("lang", "tup", None),
            P("lang", "tup"),
            P("lang", "tup"),
            P("tup", None),
            P("lang", "tup", None),
        ),
        out_specs=(P("tup", None), P("lang", "tup", None)),
        check_vma=False,
    )
```

profile of v0, /device:TPU:4, one launch (start us, length us, event | category | flops | bytes accessed | tf_op | source)
XLA Modules:
  0.0 659.9 jit_solution(987465419086488916)
XLA Ops:
  8.6 2.5 sort.17
  13.4 11.5 %all-to-all-start = ((s32[32,1,4]{2,1,0:T(1,128)}), s32[32,1,4]{2,1,0:T(1,128)S(1)}, u32[]{:S(2)}, u32[]{:S(2)}) async-start(s32[32,1,4]{2,1,0:T(1,128)} %bitcast.1), calls=%async_computation | async-start | bytes 32768 | tf_op jit(solution)/shard_map/all_to_all | solution.py:77
  24.9 5.4 compare_select_fusion
  30.3 11.5 %gather_fusion.1 = bf16[128,16384]{1,0:T(8,128)(2,1)} fusion(bf16[128,16384]{1,0:T(8,128)(2,1)} %compare_select_fusion, s32[1024]{0:T(1024)S(1)} %pad_clamp_fusion.1), kind=kCustom, calls=%fused_computation.1 | custom fusion | bytes 8389120 | tf_op jit(solution)/shard_map/gather | solution.py:71
  41.8 7.2 %reshape.96 = bf16[32,4,16384]{2,1,0:T(4,128)(2,1)} reshape(bf16[128,16384]{1,0:T(8,128)(2,1)} %gather_fusion.1) | data formatting | bytes 8388608 | tf_op jit(solution)/shard_map/reshape | solution.py:71
  49.1 10.0 %all-to-all-start.1 = ((bf16[32,4,16384]{2,1,0:T(4,128)(2,1)}), bf16[32,4,16384]{2,1,0:T(4,128)(2,1)}, u32[]{:S(2)}, u32[]{:S(2)}) async-start(bf16[32,4,16384]{2,1,0:T(4,128)(2,1)} %reshape.96), calls=%async_computation.1 | async-start | bytes 8388608 | tf_op jit(solution)/shard_map/all_to_all | solution.py:70
  61.6 130.7 %all-to-all-done.1 = bf16[32,4,16384]{2,1,0:T(4,128)(2,1)} async-done(((bf16[32,4,16384]{2,1,0:T(4,128)(2,1)}), bf16[32,4,16384]{2,1,0:T(4,128)(2,1)}, u32[]{:S(2)}, u32[]{:S(2)}) %all-to-all-start.1) | async-done | bytes 4194336 | tf_op jit(solution)/shard_map/all_to_all | solution.py:70
  192.2 6.9 %reshape.97 = bf16[128,16384]{1,0:T(8,128)(2,1)} reshape(bf16[32,4,16384]{2,1,0:T(4,128)(2,1)} %all-to-all-done.1) | data formatting | bytes 8388608 | tf_op jit(solution)/shard_map/reshape | solution.py:76
  199.2 6.0 broadcast_in_dim.7
  205.2 60.9 %while.16 = (s32[]{:T(128)}, f32[128,256]{1,0:T(8,128)S(1)}, f32[16384,256]{1,0:T(8,128)}, bf16[128,16384]{1,0:T(8,128)(2,1)}, bf16[16384,256]{1,0:T(8,128)(2,1)...) while((s32[]{:T(128)}, f32[128,256]{1,0:T(8,128)S(1)}, ...), condition=%wide.region_2.3_spmd.clone, body=%wide.region_1.2_spmd.clone.sunk | while | flops 1745420288 | bytes 10354869 | solution.py:49
  208.2 2.3 convolution_add_fusion.2
  210.4 2.3 convolution_dynamic-update-slice_fusion.2
  215.8 2.3 convolution_add_fusion.2
  218.1 2.3 convolution_dynamic-update-slice_fusion.2
  223.4 2.3 convolution_add_fusion.2
  225.6 2.3 convolution_dynamic-update-slice_fusion.2
  229.3 1.7 fusion.31
  231.0 2.3 convolution_add_fusion.2
  233.2 2.3 convolution_dynamic-update-slice_fusion.2
  236.9 1.7 fusion.31
  238.6 2.3 convolution_add_fusion.2
  240.9 2.4 convolution_dynamic-update-slice_fusion.2
  246.3 2.3 convolution_add_fusion.2
  248.5 2.3 convolution_dynamic-update-slice_fusion.2
  253.8 2.3 convolution_add_fusion.2
  256.1 2.3 convolution_dynamic-update-slice_fusion.2
  261.5 2.3 convolution_add_fusion.2
  263.7 2.3 convolution_dynamic-update-slice_fusion.2
  268.4 57.4 %all-reduce.2.cloned.1.call-done = f32[128,256]{1,0:T(8,128)} async-done(((f32[128,256]{1,0:T(8,128)}), f32[128,256]{1,0:T(8,128)}) %all-reduce.2.cloned.1.call-update) | async-done | bytes 131088 | tf_op jit(solution)/shard_map/psum | solution.py:84
  328.5 249.4 %reduce-scatter.2.cloned.1.call-done = f32[512,256]{1,0:T(8,128)} async-done(((f32[16384,256]{1,0:T(8,128)}), f32[512,256]{1,0:T(8,128)}) %reduce-scatter.2.cloned.1.call-update) | async-done | bytes 524304 | tf_op jit(solution)/shard_map/reduce_scatter | solution.py:55
  579.1 72.4 %psum.15 = f32[256]{0:T(256)S(1)} all-reduce(f32[256]{0:T(256)S(1)} %fusion.5), channel_id=1, replica_groups=mesh['tup'=32,'lang'=8] {'tup'}, use_global_device_ids=true, to_apply=%region_8.9 | all-reduce | flops 256 | bytes 2048 | tf_op jit(solution)/shard_map/psum | solution.py:88
  651.5 1.9 divide_bitcast_fusion
  (52 shorter events, 33.0 us)
Async XLA Ops:
  7.2 192.0 %all-gather.3.cloned.1.call-start = ((), (), s32[]{:S(2)}) async-start(), calls=%async_computation.5 | async-start | bytes 8650752 | tf_op jit(solution)/shard_map/all_gather | solution.py:33
  13.4 35.6 %all-to-all-start = ((s32[32,1,4]{2,1,0:T(1,128)}), s32[32,1,4]{2,1,0:T(1,128)S(1)}, u32[]{:S(2)}, u32[]{:S(2)}) async-start(s32[32,1,4]{2,1,0:T(1,128)} %bitcast.1), calls=%async_computation | async-start | bytes 32768 | tf_op jit(solution)/shard_map/all_to_all | solution.py:77
  49.1 11.6 %copy-start = (bf16[128,256]{1,0:T(8,128)(2,1)S(1)}, bf16[128,256]{1,0:T(8,128)(2,1)}, u32[]{:S(2)}) copy-start(bf16[128,256]{1,0:T(8,128)(2,1)} %param.10) | copy-start | bytes 196612
  49.1 143.2 %all-to-all-start.1 = ((bf16[32,4,16384]{2,1,0:T(4,128)(2,1)}), bf16[32,4,16384]{2,1,0:T(4,128)(2,1)}, u32[]{:S(2)}, u32[]{:S(2)}) async-start(bf16[32,4,16384]{2,1,0:T(4,128)(2,1)} %reshape.96), calls=%async_computation.1 | async-start | bytes 8388608 | tf_op jit(solution)/shard_map/all_to_all | solution.py:70
  59.1 266.7 %all-reduce.2.cloned.1.call-start = ((), (), s32[]{:S(2)}) async-start(), calls=%async_computation.3 | async-start | bytes 262144 | tf_op jit(solution)/shard_map/psum | solution.py:84
  267.7 310.2 %reduce-scatter.2.cloned.1.call-start = ((), (), s32[]{:S(2)}) async-start(), calls=%async_computation.4 | async-start | bytes 17301504 | tf_op jit(solution)/shard_map/reduce_scatter | solution.py:55
  267.7 310.2 %copy-start.1 = (bf16[1,512,256]{2,1,0:T(8,128)(2,1)S(1)}, bf16[1,512,256]{2,1,0:T(8,128)(2,1)}, u32[]{:S(2)}) copy-start(bf16[1,512,256]{2,1,0:T(8,128)(2,1)} %param.11) | copy-start | bytes 786436
Sparse Core Ops, SparseCore 0:
  10.6 176.9 all-gather.2
  267.8 57.9 all-reduce.1
  330.5 247.3 reduce-scatter.1
where the time goes:
time: 662 us; the launch traced here: 660 us
  waiting for transfers between devices  439 us (66%)
  blocking collectives  72.4 us (11%)
  matrix products  49.9 us (8%)
  local copies, waits for them, and re-layouts  47.8 us (7%)
  starting transfers between devices  21.8 us (3%)
  other arithmetic  15.1 us (2%)
  between operations  13.8 us (2%)
    reduce_scatter x1, waiting for transfers between devices, ratio_pass(): lax.psum_scatter(word_sum, 'tup', scatter_dimension=0, tiled=True)  249 us
    all_to_all x1, waiting for transfers between devices, on_device(): lax.all_to_all(live_counts[bucket_order].reshape(groups, per_owner, vocab...  131 us
    psum x1, blocking collectives, on_device(): column = lax.psum(jnp.sum(scaled, 0), 'tup')  72.4 us
    psum x1, waiting for transfers between devices, on_device(): totals = lax.psum(placed, 'lang')  57.4 us
    dot_general x8, matrix products, word_term(): lax.dot_general(ratios, mix_rows.astype(jnp.float32), (((0,), (0,)), ((),...  18.6 us
    dot_general x8, matrix products, topic_term(): jnp.dot(ratios, word_block.astype(jnp.float32), precision=lax.Precision.H...  18 us
    dot_general x8, matrix products, ratio_block(): lax.dot_general(mix_block, word_block, (((1,), (1,)), ((), ())), preferre...  13.3 us
  transfers between devices with their start and end apart: 5, of which 3 were waited for; matrix products, arithmetic and copies ran while one was open for 6% of the time, Pallas kernels for 0%

commit v1 on v0

--- a/solution.py
+++ b/solution.py
@@ -85,7 +85,7 @@
     mixed = topic_mix.astype(jnp.float32) * totals
     mix_update = topics * mixed / jnp.sum(mixed, 1, keepdims=True)
     scaled = word_local.astype(jnp.float32) * word_sum
-    column = lax.psum(jnp.sum(scaled, 0), "tup")
+    column = jnp.sum(lax.all_gather(jnp.sum(scaled, 0), "tup"), axis=0)
     word_update = (vocab_size * scaled / column[None, :])[None]
     return (mix_update, word_update)
 

time: 662 us -> 631 us (0.953)
  blocking collectives: 72.4 us -> 41.5 us
    psum x1 -> x0, blocking collectives: 72.4 us -> none  [on_device(): column = lax.psum(jnp.sum(scaled, 0), 'tup')]
    all_gather x0 -> x1, blocking collectives: none -> 41.5 us  [on_device(): column = jnp.sum(lax.all_gather(jnp.sum(scaled, 0), 'tup'), axis=0)]
where the time goes in v1:
time: 631 us; the launch traced here: 629 us
  waiting for transfers between devices  439 us (70%)
  matrix products  49.9 us (8%)
  local copies, waits for them, and re-layouts  47.8 us (8%)
  blocking collectives  41.5 us (7%)
  starting transfers between devices  21.8 us (3%)
  other arithmetic  15.1 us (2%)
  between operations  13.8 us (2%)
    reduce_scatter x1, waiting for transfers between devices, ratio_pass(): lax.psum_scatter(word_sum, 'tup', scatter_dimension=0, tiled=True)  249 us
    all_to_all x1, waiting for transfers between devices, on_device(): lax.all_to_all(live_counts[bucket_order].reshape(groups, per_owner, vocab...  131 us
    psum x1, waiting for transfers between devices, on_device(): totals = lax.psum(placed, 'lang')  57.4 us
    all_gather x1, blocking collectives, on_device(): column = jnp.sum(lax.all_gather(jnp.sum(scaled, 0), 'tup'), axis=0)  41.5 us
    dot_general x8, matrix products, word_term(): lax.dot_general(ratios, mix_rows.astype(jnp.float32), (((0,), (0,)), ((),...  18.6 us
    dot_general x8, matrix products, topic_term(): jnp.dot(ratios, word_block.astype(jnp.float32), precision=lax.Precision.H...  18 us
    dot_general x8, matrix products, ratio_block(): lax.dot_general(mix_block, word_block, (((1,), (1,)), ((), ())), preferre...  13.3 us
  transfers between devices with their start and end apart: 5, of which 3 were waited for; matrix products, arithmetic and copies ran while one was open for 6% of the time, Pallas kernels for 0%

profile of v1, /device:TPU:4, one launch (start us, length us, event | category | flops | bytes accessed | tf_op | source)
XLA Modules:
  0.0 629.1 jit_solution(13690653622821734836)
XLA Ops:
  8.6 2.5 sort.17
  13.4 11.5 %all-to-all-start = ((s32[32,1,4]{2,1,0:T(1,128)}), s32[32,1,4]{2,1,0:T(1,128)S(1)}, u32[]{:S(2)}, u32[]{:S(2)}) async-start(s32[32,1,4]{2,1,0:T(1,128)} %bitcast.1), calls=%async_computation | async-start | bytes 32768 | tf_op jit(solution)/shard_map/all_to_all | solution.py:77
  24.9 5.4 compare_select_fusion
  30.3 11.5 %gather_fusion.1 = bf16[128,16384]{1,0:T(8,128)(2,1)} fusion(bf16[128,16384]{1,0:T(8,128)(2,1)} %compare_select_fusion, s32[1024]{0:T(1024)S(1)} %pad_clamp_fusion.1), kind=kCustom, calls=%fused_computation.1 | custom fusion | bytes 8389120 | tf_op jit(solution)/shard_map/gather | solution.py:71
  41.8 7.2 %reshape.96 = bf16[32,4,16384]{2,1,0:T(4,128)(2,1)} reshape(bf16[128,16384]{1,0:T(8,128)(2,1)} %gather_fusion.1) | data formatting | bytes 8388608 | tf_op jit(solution)/shard_map/reshape | solution.py:71
  49.1 10.0 %all-to-all-start.1 = ((bf16[32,4,16384]{2,1,0:T(4,128)(2,1)}), bf16[32,4,16384]{2,1,0:T(4,128)(2,1)}, u32[]{:S(2)}, u32[]{:S(2)}) async-start(bf16[32,4,16384]{2,1,0:T(4,128)(2,1)} %reshape.96), calls=%async_computation.1 | async-start | bytes 8388608 | tf_op jit(solution)/shard_map/all_to_all | solution.py:70
  61.6 130.7 %all-to-all-done.1 = bf16[32,4,16384]{2,1,0:T(4,128)(2,1)} async-done(((bf16[32,4,16384]{2,1,0:T(4,128)(2,1)}), bf16[32,4,16384]{2,1,0:T(4,128)(2,1)}, u32[]{:S(2)}, u32[]{:S(2)}) %all-to-all-start.1) | async-done | bytes 4194336 | tf_op jit(solution)/shard_map/all_to_all | solution.py:70
  192.2 6.9 %reshape.97 = bf16[128,16384]{1,0:T(8,128)(2,1)} reshape(bf16[32,4,16384]{2,1,0:T(4,128)(2,1)} %all-to-all-done.1) | data formatting | bytes 8388608 | tf_op jit(solution)/shard_map/reshape | solution.py:76
  199.2 6.0 broadcast_in_dim.7
  205.2 60.9 %while.16 = (s32[]{:T(128)}, f32[128,256]{1,0:T(8,128)S(1)}, f32[16384,256]{1,0:T(8,128)}, bf16[128,16384]{1,0:T(8,128)(2,1)}, bf16[16384,256]{1,0:T(8,128)(2,1)...) while((s32[]{:T(128)}, f32[128,256]{1,0:T(8,128)S(1)}, ...), condition=%wide.region_2.3_spmd.clone, body=%wide.region_1.2_spmd.clone.sunk | while | flops 1745420288 | bytes 10354869 | solution.py:49
  208.2 2.3 convolution_add_fusion.2
  210.4 2.3 convolution_dynamic-update-slice_fusion.2
  215.8 2.3 convolution_add_fusion.2
  218.1 2.3 convolution_dynamic-update-slice_fusion.2
  223.4 2.3 convolution_add_fusion.2
  225.6 2.3 convolution_dynamic-update-slice_fusion.2
  229.3 1.7 fusion.31
  231.0 2.3 convolution_add_fusion.2
  233.2 2.3 convolution_dynamic-update-slice_fusion.2
  236.9 1.7 fusion.31
  238.6 2.3 convolution_add_fusion.2
  240.9 2.4 convolution_dynamic-update-slice_fusion.2
  246.3 2.3 convolution_add_fusion.2
  248.5 2.3 convolution_dynamic-update-slice_fusion.2
  253.8 2.3 convolution_add_fusion.2
  256.1 2.3 convolution_dynamic-update-slice_fusion.2
  261.5 2.3 convolution_add_fusion.2
  263.7 2.3 convolution_dynamic-update-slice_fusion.2
  268.4 57.4 %all-reduce.2.cloned.1.call-done = f32[128,256]{1,0:T(8,128)} async-done(((f32[128,256]{1,0:T(8,128)}), f32[128,256]{1,0:T(8,128)}) %all-reduce.2.cloned.1.call-update) | async-done | bytes 131088 | tf_op jit(solution)/shard_map/psum | solution.py:84
  328.5 249.4 %reduce-scatter.2.cloned.1.call-done = f32[512,256]{1,0:T(8,128)} async-done(((f32[16384,256]{1,0:T(8,128)}), f32[512,256]{1,0:T(8,128)}) %reduce-scatter.2.cloned.1.call-update) | async-done | bytes 524304 | tf_op jit(solution)/shard_map/reduce_scatter | solution.py:55
  579.1 41.5 %all-gather.2 = f32[32,1,256]{2,1,0:T(1,128)S(1)} all-gather(f32[1,1,256]{2,1,0:T(1,128)S(1)} %bitcast.37), channel_id=3, replica_groups=mesh['tup'=32,'lang'=8] {'tup'}, dimensions={0}, use_global_device_ids=true | all-gather | bytes 33792 | tf_op jit(solution)/shard_map/all_gather | solution.py:88
  620.6 1.9 divide_bitcast_fusion
  (53 shorter events, 33.1 us)
Async XLA Ops:
  7.2 192.0 %all-gather.5.cloned.1.call-start = ((), (), s32[]{:S(2)}) async-start(), calls=%async_computation.5 | async-start | bytes 8650752 | tf_op jit(solution)/shard_map/all_gather | solution.py:33
  13.4 35.6 %all-to-all-start = ((s32[32,1,4]{2,1,0:T(1,128)}), s32[32,1,4]{2,1,0:T(1,128)S(1)}, u32[]{:S(2)}, u32[]{:S(2)}) async-start(s32[32,1,4]{2,1,0:T(1,128)} %bitcast.1), calls=%async_computation | async-start | bytes 32768 | tf_op jit(solution)/shard_map/all_to_all | solution.py:77
  49.1 11.6 %copy-start = (bf16[128,256]{1,0:T(8,128)(2,1)S(1)}, bf16[128,256]{1,0:T(8,128)(2,1)}, u32[]{:S(2)}) copy-start(bf16[128,256]{1,0:T(8,128)(2,1)} %param.10) | copy-start | bytes 196612
  49.1 143.2 %all-to-all-start.1 = ((bf16[32,4,16384]{2,1,0:T(4,128)(2,1)}), bf16[32,4,16384]{2,1,0:T(4,128)(2,1)}, u32[]{:S(2)}, u32[]{:S(2)}) async-start(bf16[32,4,16384]{2,1,0:T(4,128)(2,1)} %reshape.96), calls=%async_computation.1 | async-start | bytes 8388608 | tf_op jit(solution)/shard_map/all_to_all | solution.py:70
  59.1 266.7 %all-reduce.2.cloned.1.call-start = ((), (), s32[]{:S(2)}) async-start(), calls=%async_computation.3 | async-start | bytes 262144 | tf_op jit(solution)/shard_map/psum | solution.py:84
  267.7 310.2 %reduce-scatter.2.cloned.1.call-start = ((), (), s32[]{:S(2)}) async-start(), calls=%async_computation.4 | async-start | bytes 17301504 | tf_op jit(solution)/shard_map/reduce_scatter | solution.py:55
  267.7 310.2 %copy-start.1 = (bf16[1,512,256]{2,1,0:T(8,128)(2,1)S(1)}, bf16[1,512,256]{2,1,0:T(8,128)(2,1)}, u32[]{:S(2)}) copy-start(bf16[1,512,256]{2,1,0:T(8,128)(2,1)} %param.11) | copy-start | bytes 786436
Sparse Core Ops, SparseCore 0:
  10.6 176.9 all-gather.4
  267.8 57.9 all-reduce.1
  330.5 247.3 reduce-scatter.1
